TPU v7x, 32 devices: a whole 2x2x4 slice. The times are simulated.
32 devices in a mesh: row: 8 (over z, x), col: 4 (over y, core).
Axes of the slice: x: 2, y: 2, z: 4, core: 2. Of those that a mesh axis runs over, the one named last changes fastest.
Arguments:
- records: bfloat16 [128, 8, 1500], P('row', 'col'), may hold values from -6 to 6
- channel_live: int32 [128], replicated, may hold values 0 or 1
- minute_valid: int32 [8], replicated, may hold values 0 or 1
Outputs:
- correlations: bfloat16 [128, 128, 801], P('row', 'col')
All inputs are finite; a program needn't handle non-finite values.
Results may differ from a plain program's by a relative error of at most 0.0075.
Values may be sent and summed in bfloat16 or wider, within the bound.
A program may use at most 64 MiB of HBM per device.

v0:
```python
import math
import jax
import jax.numpy as jnp
from jax import lax
from jax.sharding import PartitionSpec as P

F = 640
BAND = 32
MAXLAG = 400


def forward_table(length, nfreq):
    times = jnp.arange(length, dtype=jnp.int32)[:, None]
    freqs = jnp.arange(1, nfreq + 1, dtype=jnp.int32)[None, :]
    phase = (times * freqs % length).astype(jnp.float32) * jnp.float32(2.0 * math.pi / length)
    return jnp.concatenate([jnp.cos(phase), -jnp.sin(phase)], axis=1).astype(jnp.bfloat16)


def inverse_table(length, nfreq, maxlag):
    freqs = jnp.arange(1, nfreq + 1, dtype=jnp.int32)[:, None]
    shifts = jnp.arange(-maxlag, maxlag + 1, dtype=jnp.int32)[None, :]
    phase = jnp.mod(freqs * shifts, length).astype(jnp.float32) * jnp.float32(
        2.0 * math.pi / length
    )
    return jnp.concatenate([jnp.cos(phase), -jnp.sin(phase)], axis=0).astype(jnp.bfloat16)


def whiten(signal, live, valid, table, band):
    chans, mins, length = signal.shape
    nfreq = table.shape[1] // 2
    spectrum = jnp.dot(
        signal.reshape(chans * mins, length), table, preferred_element_type=jnp.float32
    )
    grouped = spectrum.reshape(chans, mins, 2, nfreq // band, band)
    power = jnp.mean(grouped * grouped, axis=(2, 4))
    weight = (
        lax.rsqrt(power + 1e-06)
        * live.astype(jnp.float32)[:, None, None]
        * valid.astype(jnp.float32)[None, :, None]
    )
    return (
        (grouped * weight[:, :, None, :, None]).reshape(chans, mins, 2 * nfreq).astype(jnp.bfloat16)
    )


def correlate(rows, cols, itab, count):
    nfreq = rows.shape[2] // 2
    row_real = rows[:, :, :nfreq]
    row_imag = rows[:, :, nfreq:]
    col_real = cols[:, :, :nfreq]
    col_imag = cols[:, :, nfreq:]
    real_sum = jnp.einsum(
        "imf,jmf->ijf", row_real, col_real, preferred_element_type=jnp.float32
    ) + jnp.einsum("imf,jmf->ijf", row_imag, col_imag, preferred_element_type=jnp.float32)
    imag_sum = jnp.einsum(
        "imf,jmf->ijf", row_imag, col_real, preferred_element_type=jnp.float32
    ) - jnp.einsum("imf,jmf->ijf", row_real, col_imag, preferred_element_type=jnp.float32)
    stacked = (jnp.concatenate([real_sum, imag_sum], axis=-1) / jnp.float32(count)).astype(
        jnp.bfloat16
    )
    lagged = jnp.dot(stacked.reshape(-1, 2 * nfreq), itab, preferred_element_type=jnp.float32)
    lagged = lagged * jnp.float32(1.0 / math.sqrt(nfreq))
    return lagged.astype(jnp.bfloat16).reshape(rows.shape[0], cols.shape[0], itab.shape[1])


def body(records, channel_live, minute_valid):
    row_total = lax.axis_size("row")
    col_total = lax.axis_size("col")
    row_count = records.shape[0]
    per_device = records.shape[1]
    length = records.shape[2]
    channels = row_count * row_total
    col_count = channels // col_total
    minutes = per_device * col_total
    col_index = lax.axis_index("col")
    row_start = lax.axis_index("row") * row_count
    row_live = lax.dynamic_slice_in_dim(channel_live, row_start, row_count)
    table = forward_table(length, F)
    own_valid = lax.dynamic_slice_in_dim(minute_valid, col_index * per_device, per_device)
    local = whiten(records, row_live, own_valid, table, BAND)
    row_spectra = lax.all_gather(local, "col", axis=1, tiled=True)
    every_channel = lax.all_gather(local, "row", axis=0, tiled=True)
    col_spectra = lax.all_to_all(every_channel, "col", split_axis=0, concat_axis=1, tiled=True)
    itab = inverse_table(length, F, MAXLAG)
    block = math.gcd(row_count, 8)
    grouped = row_spectra.reshape(row_count // block, block, minutes, 2 * F)

    def one_block(rows):
        return correlate(rows, col_spectra, itab, minutes)

    result = lax.map(one_block, grouped)
    return result.reshape(row_count, col_count, 2 * MAXLAG + 1)


def solution(mesh):
    in_specs = (P("row", "col", None), P(), P())
    out_specs = P("row", "col", None)
    return jax.shard_map(body, mesh=mesh, in_specs=in_specs, out_specs=out_specs, check_vma=False)
```

profile of v0, /device:TPU:0, one launch (start us, length us, event | category | flops | bytes accessed | tf_op | source)
XLA Modules:
  0.0 129.4 jit_solution(9751996412103795063)
XLA Ops:
  0.0 17.2 %cosine_convert_fusion = (bf16[1500,640]{1,0:T(8,128)(2,1)S(1)}, bf16[1500,640]{1,0:T(8,128)(2,1)}) fusion(s32[640]{0:T(1024)S(1)} %iota_add_fusion.1), kind=kLoop, calls=%fused_computation.31 | loop fusion | flops 11520000 | bytes 3842560 | tf_op jit(solution)/shard_map/convert.2
  17.3 2.3 %fusion.45 = (f32[32,1280]{1,0:T(8,128)S(1)}, f32[32,1280]{1,0:T(8,128)S(1)}) fusion(bf16[32,1500]{1,0:T(8,128)(2,1)S(1)} %reshape.42, bf16[1500,640]{1,0:T(8,128)(2,1)} %get-tuple-element.61, bf16[1500,640]{1,0:T(8,128)(2,1)S(1)} %get-tuple-element.60), kind=kOutput, calls=%fused_computation.59 | convolution fusion | flops 130600960 | bytes 4263680 | tf_op jit(solution)/shard_map/dot_general | solution.py:31
  20.9 33.5 %all_gather.7 = bf16[128,2,1280]{2,0,1:T(8,128)(2,1)S(1)} all-gather(bf16[16,2,1280]{2,0,1:T(8,128)(2,1)S(1)} %fusion.39), channel_id=1, replica_groups=mesh['row'=8,'col'=4] {'row'}, dimensions={0}, use_global_device_ids=true | all-gather | bytes 737280 | tf_op jit(solution)/shard_map/all_gather | solution.py:82
  54.4 1.5 %copy.28 = bf16[128,2,1280]{2,1,0:T(2,128)(2,1)} copy(bf16[128,2,1280]{2,0,1:T(8,128)(2,1)S(1)} %all_gather.7) | data formatting | bytes 1310720 | tf_op jit(solution)/shard_map/all_gather | solution.py:82
  55.9 3.5 %all-to-all-start = ((bf16[128,2,1280]{2,1,0:T(2,128)(2,1)}), bf16[128,2,1280]{2,1,0:T(2,128)(2,1)S(1)}, u32[]{:S(2)}, u32[]{:S(2)}) async-start(bf16[128,2,1280]{2,1,0:T(2,128)(2,1)} %copy.28), calls=%async_computation | async-start | bytes 1310720 | tf_op jit(solution)/shard_map/all_to_all | solution.py:83
  59.4 10.2 %cosine_convert_fusion.1 = (bf16[640,801]{1,0:T(8,128)(2,1)S(1)}, bf16[640,801]{1,0:T(8,128)(2,1)S(1)}) fusion(s32[801]{0:T(1024)S(1)} %iota_add_fusion, s32[640]{0:T(1024)S(1)} %iota_add_fusion.1), kind=kLoop, calls=%fused_computation.41 | loop fusion | flops 6151680 | bytes 2056324 | tf_op jit(solution)/shard_map/convert
  69.6 6.8 %all_gather.6 = bf16[16,8,1280]{2,0,1:T(8,128)(2,1)S(1)} all-gather(bf16[16,2,1280]{2,0,1:T(8,128)(2,1)S(1)} %fusion.39), channel_id=1, replica_groups=mesh['row'=8,'col'=4] {'col'}, dimensions={1}, use_global_device_ids=true | all-gather | bytes 409600 | tf_op jit(solution)/shard_map/all_gather | solution.py:81
  76.4 1.6 %pad_maximum_fusion = bf16[1280,801]{1,0:T(8,128)(2,1)} fusion(bf16[640,801]{1,0:T(8,128)(2,1)S(1)} %get-tuple-element.59, bf16[640,801]{1,0:T(8,128)(2,1)S(1)} %get-tuple-element.58), kind=kLoop, calls=%fused_computation.39 | loop fusion | flops 4101120 | bytes 4101120 | tf_op jit(solution)/shard_map/concatenate | solution.py:25
  78.0 4.9 %copy.29 = bf16[32,4,2,1280]{0,2,1,3:T(2,128)(2,1)} copy(bf16[32,4,2,1280]{3,2,0,1:T(2,128)(2,1)S(1)} %bitcast.75) | data formatting | bytes 1310720 | tf_op jit(solution)/shard_map/all_to_all | solution.py:83
  82.9 46.5 %while.10 = (s32[]{:T(128)}, bf16[2,8,32,801]{3,2,1,0:T(8,128)(2,1)}, bf16[2,8,8,1280]{3,1,0,2:T(8,128)(2,1)S(1)}, bf16[32,8,1280]{0,1,2:T(8,128)(2,1)}, bf16[1280,801]{1,0:T(8,128)(2,1)}, /*index=5*/s32[]{:T(128)}) while((s32[]{:T(128)}, bf16[2,8,32,801]{3,2,1,0:T(8,128)(2,1)}, bf16[2,8,8,1280]{3,1,0,2:T(8,128)(2,1)S(1)}, ...), condition=%wide.region_2.3_spmd, body=%wide.region_1.2_spmd.sunk | while | flops 537149952 | bytes 34353424 | solution.py:91
  83.7 1.8 %copy.50 = bf16[1,8,8,1280]{2,1,3,0:T(8,128)(2,1)S(1)} copy(bf16[1,8,8,1280]{3,1,0,2:T(8,128)(2,1)S(1)} %constant_dynamic-slice_fusion.2) | data formatting | bytes 327680 | tf_op jit(solution)/shard_map/while/body/jit(dynamic_index_in_dim)/dynamic_slice | solution.py:91
  85.4 1.4 %fusion.98 = bf16[32,8,640]{0,1,2:T(8,128)(2,1)S(1)} fusion(bf16[32,8,1280]{0,1,2:T(8,128)(2,1)} %get-tuple-element.110), kind=kLoop, calls=%fused_computation.15.clone.1.clone.1 | loop fusion | bytes 655360 | tf_op jit(solution)/shard_map/while/body/eval_jaxpr/imf,jmf->ijf/dot_general | solution.py:54
  87.7 0.9 copy-done
  88.7 2.4 %add_bitcast_fusion.2 = f32[8,32,640]{1,0,2:T(8,128)} fusion(f32[640,8,32]{2,1,0:T(8,128)S(1)} %fusion.99, bf16[1,8,8,1280]{2,1,3,0:T(8,128)(2,1)S(1)} %copy.50, bf16[32,8,640]{0,1,2:T(8,128)(2,1)S(1)} %fusion.100), kind=kOutput, calls=%fused_computation.9.clone.2 | convolution fusion | flops 2785280 | bytes 1802240 | tf_op jit(solution)/shard_map/while/body/eval_jaxpr/imf,jmf->ijf/dot_general | solution.py:52
  91.0 3.0 %copy.52 = f32[8,32,640]{2,1,0:T(8,128)} copy(f32[8,32,640]{1,0,2:T(8,128)} %add_bitcast_fusion.2) | data formatting | bytes 1310720 | tf_op jit(solution)/shard_map/while/body/eval_jaxpr/add | solution.py:52
  94.1 1.4 %fusion.95 = bf16[32,8,640]{0,1,2:T(8,128)(2,1)S(1)} fusion(bf16[32,8,1280]{0,1,2:T(8,128)(2,1)} %get-tuple-element.110), kind=kLoop, calls=%fused_computation.16.clone.1.clone.1 | loop fusion | bytes 655360 | tf_op jit(solution)/shard_map/while/body/eval_jaxpr/imf,jmf->ijf/dot_general | solution.py:55
  96.3 0.9 copy-done.1
  97.3 2.4 %subtract_bitcast_fusion.2 = f32[8,32,640]{1,0,2:T(8,128)} fusion(f32[640,8,32]{2,1,0:T(8,128)S(1)} %fusion.96, bf16[1,8,8,1280]{2,1,3,0:T(8,128)(2,1)S(1)} %copy.50, bf16[32,8,640]{0,1,2:T(8,128)(2,1)S(1)} %fusion.97), kind=kOutput, calls=%fused_computation.8.clone.2 | convolution fusion | flops 2785280 | bytes 1802240 | tf_op jit(solution)/shard_map/while/body/eval_jaxpr/imf,jmf->ijf/dot_general | solution.py:57
  99.7 2.5 %copy.51 = f32[8,32,640]{2,1,0:T(8,128)S(1)} copy(f32[8,32,640]{1,0,2:T(8,128)} %subtract_bitcast_fusion.2) | data formatting | bytes 1310720 | tf_op jit(solution)/shard_map/while/body/eval_jaxpr/sub | solution.py:55
  102.2 2.7 %fusion.101 = bf16[256,801]{0,1:T(8,128)(2,1)S(1)} fusion(bf16[1280,801]{1,0:T(8,128)(2,1)} %get-tuple-element.111, f32[256,640]{1,0:T(8,128)S(1)} %bitcast.73, f32[256,640]{1,0:T(8,128)S(1)} %bitcast.72), kind=kOutput, calls=%fused_computation.13.clone.1 | convolution fusion | flops 526336512 | bytes 3771392 | tf_op jit(solution)/shard_map/while/body/eval_jaxpr/dot_general | solution.py:61
  105.2 0.9 copy-done.7
  106.9 1.8 %copy.50 = bf16[1,8,8,1280]{2,1,3,0:T(8,128)(2,1)S(1)} copy(bf16[1,8,8,1280]{3,1,0,2:T(8,128)(2,1)S(1)} %constant_dynamic-slice_fusion.2) | data formatting | bytes 327680 | tf_op jit(solution)/shard_map/while/body/jit(dynamic_index_in_dim)/dynamic_slice | solution.py:91
  108.7 1.4 %fusion.98 = bf16[32,8,640]{0,1,2:T(8,128)(2,1)S(1)} fusion(bf16[32,8,1280]{0,1,2:T(8,128)(2,1)} %get-tuple-element.110), kind=kLoop, calls=%fused_computation.15.clone.1.clone.1 | loop fusion | bytes 655360 | tf_op jit(solution)/shard_map/while/body/eval_jaxpr/imf,jmf->ijf/dot_general | solution.py:54
  110.9 0.9 copy-done
  111.9 2.4 %add_bitcast_fusion.2 = f32[8,32,640]{1,0,2:T(8,128)} fusion(f32[640,8,32]{2,1,0:T(8,128)S(1)} %fusion.99, bf16[1,8,8,1280]{2,1,3,0:T(8,128)(2,1)S(1)} %copy.50, bf16[32,8,640]{0,1,2:T(8,128)(2,1)S(1)} %fusion.100), kind=kOutput, calls=%fused_computation.9.clone.2 | convolution fusion | flops 2785280 | bytes 1802240 | tf_op jit(solution)/shard_map/while/body/eval_jaxpr/imf,jmf->ijf/dot_general | solution.py:52
  114.3 3.0 %copy.52 = f32[8,32,640]{2,1,0:T(8,128)} copy(f32[8,32,640]{1,0,2:T(8,128)} %add_bitcast_fusion.2) | data formatting | bytes 1310720 | tf_op jit(solution)/shard_map/while/body/eval_jaxpr/add | solution.py:52
  117.3 1.4 %fusion.95 = bf16[32,8,640]{0,1,2:T(8,128)(2,1)S(1)} fusion(bf16[32,8,1280]{0,1,2:T(8,128)(2,1)} %get-tuple-element.110), kind=kLoop, calls=%fused_computation.16.clone.1.clone.1 | loop fusion | bytes 655360 | tf_op jit(solution)/shard_map/while/body/eval_jaxpr/imf,jmf->ijf/dot_general | solution.py:55
  119.6 0.9 copy-done.1
  120.6 2.4 %subtract_bitcast_fusion.2 = f32[8,32,640]{1,0,2:T(8,128)} fusion(f32[640,8,32]{2,1,0:T(8,128)S(1)} %fusion.96, bf16[1,8,8,1280]{2,1,3,0:T(8,128)(2,1)S(1)} %copy.50, bf16[32,8,640]{0,1,2:T(8,128)(2,1)S(1)} %fusion.97), kind=kOutput, calls=%fused_computation.8.clone.2 | convolution fusion | flops 2785280 | bytes 1802240 | tf_op jit(solution)/shard_map/while/body/eval_jaxpr/imf,jmf->ijf/dot_general | solution.py:57
  122.9 2.5 %copy.51 = f32[8,32,640]{2,1,0:T(8,128)S(1)} copy(f32[8,32,640]{1,0,2:T(8,128)} %subtract_bitcast_fusion.2) | data formatting | bytes 1310720 | tf_op jit(solution)/shard_map/while/body/eval_jaxpr/sub | solution.py:55
  125.5 2.7 %fusion.101 = bf16[256,801]{0,1:T(8,128)(2,1)S(1)} fusion(bf16[1280,801]{1,0:T(8,128)(2,1)} %get-tuple-element.111, f32[256,640]{1,0:T(8,128)S(1)} %bitcast.73, f32[256,640]{1,0:T(8,128)S(1)} %bitcast.72), kind=kOutput, calls=%fused_computation.13.clone.1 | convolution fusion | flops 526336512 | bytes 3771392 | tf_op jit(solution)/shard_map/while/body/eval_jaxpr/dot_general | solution.py:61
  128.5 0.9 copy-done.7
  (56 shorter events, 7.1 us)
Async XLA Ops:
  0.0 17.2 %copy-start.5 = (bf16[16,2,1500]{2,1,0:T(2,128)(2,1)S(1)}, bf16[16,2,1500]{2,1,0:T(2,128)(2,1)}, u32[]{:S(2)}) copy-start(bf16[16,2,1500]{2,1,0:T(2,128)(2,1)} %param.5) | copy-start | bytes 288004
  17.3 2.6 %copy-start.8 = (s32[128]{0:T(128)S(1)}, s32[128]{0:T(128)}, u32[]{:S(2)}) copy-start(s32[128]{0:T(128)} %param.6) | copy-start | bytes 1540
  17.3 2.7 %copy-start.9 = (s32[8]{0:T(128)S(1)}, s32[8]{0:T(128)}, u32[]{:S(2)}) copy-start(s32[8]{0:T(128)} %param.7) | copy-start | bytes 100
  55.9 22.1 %all-to-all-start = ((bf16[128,2,1280]{2,1,0:T(2,128)(2,1)}), bf16[128,2,1280]{2,1,0:T(2,128)(2,1)S(1)}, u32[]{:S(2)}, u32[]{:S(2)}) async-start(bf16[128,2,1280]{2,1,0:T(2,128)(2,1)} %copy.28), calls=%async_computation | async-start | bytes 1310720 | tf_op jit(solution)/shard_map/all_to_all | solution.py:83
  82.9 0.8 copy-start.3
  86.8 1.7 %copy-start = (bf16[32,8,1280]{0,1,2:T(8,128)(2,1)S(1)}, bf16[32,8,1280]{0,1,2:T(8,128)(2,1)}, u32[]{:S(2)}) copy-start(bf16[32,8,1280]{0,1,2:T(8,128)(2,1)} %get-tuple-element.110) | copy-start | bytes 1966084 | tf_op jit(solution)/shard_map/while
  95.5 1.7 %copy-start.1 = (bf16[32,8,1280]{0,1,2:T(8,128)(2,1)S(1)}, bf16[32,8,1280]{0,1,2:T(8,128)(2,1)}, u32[]{:S(2)}) copy-start(bf16[32,8,1280]{0,1,2:T(8,128)(2,1)} %get-tuple-element.110) | copy-start | bytes 1966084 | tf_op jit(solution)/shard_map/while
  99.7 2.5 %copy-start.2 = (f32[8,32,640]{2,1,0:T(8,128)S(1)}, f32[8,32,640]{2,1,0:T(8,128)}, u32[]{:S(2)}) copy-start(f32[8,32,640]{2,1,0:T(8,128)} %copy.52) | copy-start | bytes 1966084 | tf_op jit(solution)/shard_map/while
  102.2 3.0 %copy-start.6 = (bf16[2,8,32,801]{3,2,1,0:T(8,128)(2,1)S(1)}, bf16[2,8,32,801]{3,2,1,0:T(8,128)(2,1)}, u32[]{:S(2)}) copy-start(bf16[2,8,32,801]{3,2,1,0:T(8,128)(2,1)} %get-tuple-element.102) | copy-start | bytes 2460676 | tf_op jit(solution)/shard_map/while
  102.2 4.0 %copy-start.4 = (bf16[2,8,8,1280]{3,1,0,2:T(8,128)(2,1)S(1)}, bf16[2,8,8,1280]{3,1,0,2:T(8,128)(2,1)}, u32[]{:S(2)}) copy-start(bf16[2,8,8,1280]{3,1,0,2:T(8,128)(2,1)} %copy-done.3) | copy-start | bytes 983044 | tf_op jit(solution)/shard_map/while
  105.2 0.9 copy-start.7
  106.2 0.8 copy-start.3
  110.1 1.7 %copy-start = (bf16[32,8,1280]{0,1,2:T(8,128)(2,1)S(1)}, bf16[32,8,1280]{0,1,2:T(8,128)(2,1)}, u32[]{:S(2)}) copy-start(bf16[32,8,1280]{0,1,2:T(8,128)(2,1)} %get-tuple-element.110) | copy-start | bytes 1966084 | tf_op jit(solution)/shard_map/while
  118.7 1.7 %copy-start.1 = (bf16[32,8,1280]{0,1,2:T(8,128)(2,1)S(1)}, bf16[32,8,1280]{0,1,2:T(8,128)(2,1)}, u32[]{:S(2)}) copy-start(bf16[32,8,1280]{0,1,2:T(8,128)(2,1)} %get-tuple-element.110) | copy-start | bytes 1966084 | tf_op jit(solution)/shard_map/while
  122.9 2.5 %copy-start.2 = (f32[8,32,640]{2,1,0:T(8,128)S(1)}, f32[8,32,640]{2,1,0:T(8,128)}, u32[]{:S(2)}) copy-start(f32[8,32,640]{2,1,0:T(8,128)} %copy.52) | copy-start | bytes 1966084 | tf_op jit(solution)/shard_map/while
  125.4 3.0 %copy-start.6 = (bf16[2,8,32,801]{3,2,1,0:T(8,128)(2,1)S(1)}, bf16[2,8,32,801]{3,2,1,0:T(8,128)(2,1)}, u32[]{:S(2)}) copy-start(bf16[2,8,32,801]{3,2,1,0:T(8,128)(2,1)} %get-tuple-element.102) | copy-start | bytes 2460676 | tf_op jit(solution)/shard_map/while
  125.4 4.0 %copy-start.4 = (bf16[2,8,8,1280]{3,1,0,2:T(8,128)(2,1)S(1)}, bf16[2,8,8,1280]{3,1,0,2:T(8,128)(2,1)}, u32[]{:S(2)}) copy-start(bf16[2,8,8,1280]{3,1,0,2:T(8,128)(2,1)} %copy-done.3) | copy-start | bytes 983044 | tf_op jit(solution)/shard_map/while
  128.5 0.9 copy-start.7
where the time goes:
time: 130 us; the launch traced here: 129 us
  blocking collectives  40.2 us (31%)
  local copies, waits for them, and re-layouts  35.4 us (27%)
  other arithmetic  29.5 us (23%)
  matrix products  20.4 us (16%)
  starting transfers between devices  3.48 us (3%)
    all_gather x1, blocking collectives, body(): every_channel = lax.all_gather(local, 'row', axis=0, tiled=True)  33.5 us
    another operation x2, other arithmetic  27.4 us
    while x28, local copies, waits for them, and re-layouts  7.03 us
    all_gather x1, blocking collectives, body(): row_spectra = lax.all_gather(local, 'col', axis=1, tiled=True)  6.76 us
    add x2, local copies, waits for them, and re-layouts, correlate(): jnp.einsum('imf,jmf->ijf', row_real, col_real, preferred_element_type=jnp...  6.06 us
    dot_general x2, matrix products, correlate(): jnp.dot(stacked.reshape(-1, 2 * nfreq), itab, preferred_element_type=jnp....  5.41 us
    sub x2, local copies, waits for them, and re-layouts, correlate(): jnp.einsum('imf,jmf->ijf', row_imag, col_real, preferred_element_type=jnp...  4.94 us
    all_to_all x1, local copies, waits for them, and re-layouts, body(): lax.all_to_all(every_channel, 'col', split_axis=0, concat_axis=1, tiled=T...  4.91 us
  transfers between devices with their start and end apart: 1, of which 0 were waited for; matrix products, arithmetic and copies ran while one was open for 9% of the time, Pallas kernels for 0%

commit v1 on v0

--- a/solution.py
+++ b/solution.py
@@ -80,7 +80,19 @@
     local = whiten(records, row_live, own_valid, table, BAND)
     row_spectra = lax.all_gather(local, "col", axis=1, tiled=True)
     every_channel = lax.all_gather(local, "row", axis=0, tiled=True)
-    col_spectra = lax.all_to_all(every_channel, "col", split_axis=0, concat_axis=1, tiled=True)
+    ways, here = (lax.axis_size("col"), lax.axis_index("col"))
+    width = every_channel.shape[0] // ways
+    lengths = list(every_channel.shape)
+    lengths[0] = width
+    height = lengths[1]
+    lengths[1] = height * ways
+    full = jnp.zeros(lengths, every_channel.dtype)
+    for mask in range(ways):
+        part = lax.dynamic_slice_in_dim(every_channel, (here ^ mask) * width, width, axis=0)
+        if mask:
+            part = lax.ppermute(part, "col", [(d, d ^ mask) for d in range(ways)])
+        full = lax.dynamic_update_slice_in_dim(full, part, (here ^ mask) * height, axis=1)
+    col_spectra = full
     itab = inverse_table(length, F, MAXLAG)
     block = math.gcd(row_count, 8)
     grouped = row_spectra.reshape(row_count // block, block, minutes, 2 * F)

time: 130 us -> 142 us (1.092)
  local copies, waits for them, and re-layouts: 35.4 us -> 46.4 us
  matrix products: 20.4 us -> 22.4 us
  starting transfers between devices: 3.48 us -> 1.86 us
    all_to_all x1 -> x0, local copies, waits for them, and re-layouts: 4.91 us -> none  [body(): lax.all_to_all(every_channel, 'col', split_axis=0, concat_axis=1, tiled=T...]
    ppermute x0 -> x3, local copies, waits for them, and re-layouts: none -> 4.03 us  [body(): part = lax.ppermute(part, 'col', [(d, d ^ mask) for d in range(ways)])]
    while x28 -> x12, local copies, waits for them, and re-layouts: 7.03 us -> 3.04 us
    dynamic_update_slice x0 -> x4, local copies, waits for them, and re-layouts: none -> 3.84 us  [body(): lax.dynamic_update_slice_in_dim(full, part, (here ^ mask) * height, axis=1)]
    all_to_all x1 -> x0, starting transfers between devices: 3.48 us -> none  [body(): lax.all_to_all(every_channel, 'col', split_axis=0, concat_axis=1, tiled=T...]
    dot_general x2, local copies, waits for them, and re-layouts: 0.17 us -> 2.81 us  [correlate(): jnp.einsum('imf,jmf->ijf', row_real, col_imag, preferred_element_type=jnp...]
    dot_general x2, local copies, waits for them, and re-layouts: 0.17 us -> 2.8 us  [correlate(): jnp.einsum('imf,jmf->ijf', row_real, col_real, preferred_element_type=jnp...]
    convert_element_type x2, local copies, waits for them, and re-layouts: 0.49 us -> 2.5 us  [correlate(): lagged.astype(jnp.bfloat16)]
  transfers between devices with their start and end apart: 1 -> 3, of which waited for: 0 -> 0; matrix products, arithmetic and copies ran while one was open for 9% -> 13% of each run, Pallas kernels for 0% -> 0%
where the time goes in v1:
time: 142 us; the launch traced here: 141 us
  local copies, waits for them, and re-layouts  46.4 us (33%)
  blocking collectives  40.4 us (28%)
  other arithmetic  29.5 us (21%)
  matrix products  22.4 us (16%)
  starting transfers between devices  1.86 us (1%)
    all_gather x1, blocking collectives, body(): every_channel = lax.all_gather(local, 'row', axis=0, tiled=True)  33.6 us
    another operation x2, other arithmetic  27.4 us
    dot_general x2, matrix products, correlate(): jnp.dot(stacked.reshape(-1, 2 * nfreq), itab, preferred_element_type=jnp....  7.41 us
    all_gather x1, blocking collectives, body(): row_spectra = lax.all_gather(local, 'col', axis=1, tiled=True)  6.79 us
    sub x2, local copies, waits for them, and re-layouts, correlate(): jnp.einsum('imf,jmf->ijf', row_imag, col_real, preferred_element_type=jnp...  6.25 us
    add x2, local copies, waits for them, and re-layouts, correlate(): jnp.einsum('imf,jmf->ijf', row_real, col_real, preferred_element_type=jnp...  6.08 us
    dynamic_slice x4, local copies, waits for them, and re-layouts, body(): result = lax.map(one_block, grouped)  5.37 us
    dot_general x2, matrix products, correlate(): jnp.einsum('imf,jmf->ijf', row_real, col_imag, preferred_element_type=jnp...  4.73 us
  transfers between devices with their start and end apart: 3, of which 0 were waited for; matrix products, arithmetic and copies ran while one was open for 13% of the time, Pallas kernels for 0%

profile of v1, /device:TPU:0, one launch (start us, length us, event | category | flops | bytes accessed | tf_op | source)
XLA Modules:
  0.0 140.8 jit_solution(2500571104201167020)
XLA Ops:
  0.0 17.2 %cosine_convert_fusion = (bf16[1500,640]{1,0:T(8,128)(2,1)S(1)}, bf16[1500,640]{1,0:T(8,128)(2,1)}) fusion(s32[640]{0:T(1024)S(1)} %iota_add_fusion.1), kind=kLoop, calls=%fused_computation.31 | loop fusion | flops 11520000 | bytes 3842560 | tf_op jit(solution)/shard_map/convert.2
  17.3 2.3 %fusion.45 = (f32[32,1280]{1,0:T(8,128)S(1)}, f32[32,1280]{1,0:T(8,128)S(1)}) fusion(bf16[32,1500]{1,0:T(8,128)(2,1)S(1)} %reshape.42, bf16[1500,640]{1,0:T(8,128)(2,1)} %get-tuple-element.70, bf16[1500,640]{1,0:T(8,128)(2,1)S(1)} %get-tuple-element.69), kind=kOutput, calls=%fused_computation.67 | convolution fusion | flops 130600960 | bytes 4263680 | tf_op jit(solution)/shard_map/dot_general | solution.py:31
  20.9 33.6 %all_gather.7 = bf16[128,2,1280]{2,0,1:T(8,128)(2,1)S(1)} all-gather(bf16[16,2,1280]{2,0,1:T(8,128)(2,1)S(1)} %fusion.39), channel_id=1, replica_groups=mesh['row'=8,'col'=4] {'row'}, dimensions={0}, use_global_device_ids=true | all-gather | bytes 737280 | tf_op jit(solution)/shard_map/all_gather | solution.py:82
  55.2 1.5 %collective-permute-start.1 = (bf16[32,2,1280]{2,0,1:T(8,128)(2,1)}, bf16[32,2,1280]{2,0,1:T(8,128)(2,1)}, u32[]{:S(2)}, u32[]{:S(2)}) collective-permute-start(bf16[32,2,1280]{2,0,1:T(8,128)(2,1)} %get-tuple-element.64), channel_id=1, source_target_pairs={{0,2},{1,3},{2,0},{3,1},{4,6},{5,7},{6,4},{7,5},{8,10},{9,11},{10,... | collective-permute-start | bytes 491528 | tf_op jit(solution)/shard_map/ppermute | solution.py:93
  57.6 10.2 %cosine_convert_fusion.1 = (bf16[640,801]{1,0:T(8,128)(2,1)S(1)}, bf16[640,801]{1,0:T(8,128)(2,1)S(1)}) fusion(s32[801]{0:T(1024)S(1)} %iota_add_fusion, s32[640]{0:T(1024)S(1)} %iota_add_fusion.1), kind=kLoop, calls=%fused_computation.41 | loop fusion | flops 6151680 | bytes 2056324 | tf_op jit(solution)/shard_map/convert
  67.8 1.6 %pad_maximum_fusion = bf16[1280,801]{1,0:T(8,128)(2,1)} fusion(bf16[640,801]{1,0:T(8,128)(2,1)S(1)} %get-tuple-element.68, bf16[640,801]{1,0:T(8,128)(2,1)S(1)} %get-tuple-element.67), kind=kLoop, calls=%fused_computation.39 | loop fusion | flops 4101120 | bytes 4101120 | tf_op jit(solution)/shard_map/concatenate | solution.py:25
  70.7 6.8 %all_gather.6 = bf16[16,8,1280]{2,0,1:T(8,128)(2,1)} all-gather(bf16[16,2,1280]{2,0,1:T(8,128)(2,1)S(1)} %fusion.39), channel_id=1, replica_groups=mesh['row'=8,'col'=4] {'col'}, dimensions={1}, use_global_device_ids=true | all-gather | bytes 409600 | tf_op jit(solution)/shard_map/all_gather | solution.py:81
  79.9 1.3 copy.43
  82.2 1.3 copy.44
  84.5 56.3 %while.10 = (s32[]{:T(128)}, bf16[2,8,32,801]{3,2,1,0:T(8,128)(2,1)}, bf16[2,8,8,1280]{3,1,0,2:T(8,128)(2,1)}, bf16[32,8,1280]{0,1,2:T(8,128)(2,1)S(1)}, bf16[1280,801]{1,0:T(8,128)(2,1)}, /*index=5*/s32[]{:T(128)}) while((s32[]{:T(128)}, bf16[2,8,32,801]{3,2,1,0:T(8,128)(2,1)}, bf16[2,8,8,1280]{3,1,0,2:T(8,128)(2,1)}, ...), condition=%wide.region_2.3_spmd, body=%wide.region_1.2_spmd.sunk | while | flops 537149952 | bytes 25121948 | solution.py:103
  84.5 1.5 %copy-done = bf16[32,8,1280]{0,1,2:T(8,128)(2,1)} copy-done((bf16[32,8,1280]{0,1,2:T(8,128)(2,1)}, bf16[32,8,1280]{0,1,2:T(8,128)(2,1)S(1)}, u32[]{:S(2)}) %copy-start) | copy-done | bytes 655384 | tf_op jit(solution)/shard_map/while
  87.0 1.8 %copy.65 = bf16[1,8,8,1280]{2,1,3,0:T(8,128)(2,1)S(1)} copy(bf16[1,8,8,1280]{3,1,0,2:T(8,128)(2,1)S(1)} %constant_dynamic-slice_fusion.6) | data formatting | bytes 327680 | tf_op jit(solution)/shard_map/while/body/jit(dynamic_index_in_dim)/dynamic_slice | solution.py:103
  88.7 1.4 fusion.98
  91.0 1.4 fusion.100
  92.4 2.4 %add_bitcast_fusion.2 = f32[8,32,640]{1,0,2:T(8,128)} fusion(f32[640,8,32]{2,1,0:T(8,128)S(1)} %fusion.99, bf16[1,8,8,1280]{2,1,3,0:T(8,128)(2,1)S(1)} %copy.65, bf16[32,8,640]{0,1,2:T(8,128)(2,1)S(1)} %fusion.100), kind=kOutput, calls=%fused_computation.9.clone.2 | convolution fusion | flops 2785280 | bytes 1802240 | tf_op jit(solution)/shard_map/while/body/eval_jaxpr/imf,jmf->ijf/dot_general | solution.py:52
  94.7 3.0 %copy.67 = f32[8,32,640]{2,1,0:T(8,128)} copy(f32[8,32,640]{1,0,2:T(8,128)} %add_bitcast_fusion.2) | data formatting | bytes 1310720 | tf_op jit(solution)/shard_map/while/body/eval_jaxpr/add | solution.py:52
  97.8 1.4 fusion.95
  100.0 1.4 fusion.97
  101.4 2.4 %subtract_bitcast_fusion.2 = f32[8,32,640]{1,0,2:T(8,128)} fusion(f32[640,8,32]{2,1,0:T(8,128)S(1)} %fusion.96, bf16[1,8,8,1280]{2,1,3,0:T(8,128)(2,1)S(1)} %copy.65, bf16[32,8,640]{0,1,2:T(8,128)(2,1)S(1)} %fusion.97), kind=kOutput, calls=%fused_computation.8.clone.2 | convolution fusion | flops 2785280 | bytes 1802240 | tf_op jit(solution)/shard_map/while/body/eval_jaxpr/imf,jmf->ijf/dot_general | solution.py:57
  103.8 3.1 %copy.66 = f32[8,32,640]{2,1,0:T(8,128)} copy(f32[8,32,640]{1,0,2:T(8,128)} %subtract_bitcast_fusion.2) | data formatting | bytes 1310720 | tf_op jit(solution)/shard_map/while/body/eval_jaxpr/sub | solution.py:55
  106.9 3.7 %fusion.101 = bf16[256,801]{0,1:T(8,128)(2,1)} fusion(bf16[1280,801]{1,0:T(8,128)(2,1)} %get-tuple-element.120, f32[256,640]{1,0:T(8,128)} %bitcast.68, f32[256,640]{1,0:T(8,128)S(1)} %bitcast.67), kind=kOutput, calls=%fused_computation.13.clone.1 | convolution fusion | flops 526336512 | bytes 3771392 | tf_op jit(solution)/shard_map/while/body/eval_jaxpr/dot_general | solution.py:61
  112.7 1.5 %copy-done = bf16[32,8,1280]{0,1,2:T(8,128)(2,1)} copy-done((bf16[32,8,1280]{0,1,2:T(8,128)(2,1)}, bf16[32,8,1280]{0,1,2:T(8,128)(2,1)S(1)}, u32[]{:S(2)}) %copy-start) | copy-done | bytes 655384 | tf_op jit(solution)/shard_map/while
  115.1 1.8 %copy.65 = bf16[1,8,8,1280]{2,1,3,0:T(8,128)(2,1)S(1)} copy(bf16[1,8,8,1280]{3,1,0,2:T(8,128)(2,1)S(1)} %constant_dynamic-slice_fusion.6) | data formatting | bytes 327680 | tf_op jit(solution)/shard_map/while/body/jit(dynamic_index_in_dim)/dynamic_slice | solution.py:103
  116.9 1.4 fusion.98
  119.1 1.4 fusion.100
  120.5 2.4 %add_bitcast_fusion.2 = f32[8,32,640]{1,0,2:T(8,128)} fusion(f32[640,8,32]{2,1,0:T(8,128)S(1)} %fusion.99, bf16[1,8,8,1280]{2,1,3,0:T(8,128)(2,1)S(1)} %copy.65, bf16[32,8,640]{0,1,2:T(8,128)(2,1)S(1)} %fusion.100), kind=kOutput, calls=%fused_computation.9.clone.2 | convolution fusion | flops 2785280 | bytes 1802240 | tf_op jit(solution)/shard_map/while/body/eval_jaxpr/imf,jmf->ijf/dot_general | solution.py:52
  122.9 3.0 %copy.67 = f32[8,32,640]{2,1,0:T(8,128)} copy(f32[8,32,640]{1,0,2:T(8,128)} %add_bitcast_fusion.2) | data formatting | bytes 1310720 | tf_op jit(solution)/shard_map/while/body/eval_jaxpr/add | solution.py:52
  125.9 1.4 fusion.95
  128.2 1.4 fusion.97
  129.6 2.4 %subtract_bitcast_fusion.2 = f32[8,32,640]{1,0,2:T(8,128)} fusion(f32[640,8,32]{2,1,0:T(8,128)S(1)} %fusion.96, bf16[1,8,8,1280]{2,1,3,0:T(8,128)(2,1)S(1)} %copy.65, bf16[32,8,640]{0,1,2:T(8,128)(2,1)S(1)} %fusion.97), kind=kOutput, calls=%fused_computation.8.clone.2 | convolution fusion | flops 2785280 | bytes 1802240 | tf_op jit(solution)/shard_map/while/body/eval_jaxpr/imf,jmf->ijf/dot_general | solution.py:57
  131.9 3.1 %copy.66 = f32[8,32,640]{2,1,0:T(8,128)} copy(f32[8,32,640]{1,0,2:T(8,128)} %subtract_bitcast_fusion.2) | data formatting | bytes 1310720 | tf_op jit(solution)/shard_map/while/body/eval_jaxpr/sub | solution.py:55
  135.1 3.7 %fusion.101 = bf16[256,801]{0,1:T(8,128)(2,1)} fusion(bf16[1280,801]{1,0:T(8,128)(2,1)} %get-tuple-element.120, f32[256,640]{1,0:T(8,128)} %bitcast.68, f32[256,640]{1,0:T(8,128)S(1)} %bitcast.67), kind=kOutput, calls=%fused_computation.13.clone.1 | convolution fusion | flops 526336512 | bytes 3771392 | tf_op jit(solution)/shard_map/while/body/eval_jaxpr/dot_general | solution.py:61
  (52 shorter events, 17.7 us)
Async XLA Ops:
  0.0 17.2 %copy-start.3 = (bf16[16,2,1500]{2,1,0:T(2,128)(2,1)S(1)}, bf16[16,2,1500]{2,1,0:T(2,128)(2,1)}, u32[]{:S(2)}) copy-start(bf16[16,2,1500]{2,1,0:T(2,128)(2,1)} %param.5) | copy-start | bytes 288004
  17.3 2.6 %copy-start.4 = (s32[8]{0:T(128)S(1)}, s32[8]{0:T(128)}, u32[]{:S(2)}) copy-start(s32[8]{0:T(128)} %param.7) | copy-start | bytes 100
  17.3 2.7 %copy-start.5 = (s32[128]{0:T(128)S(1)}, s32[128]{0:T(128)}, u32[]{:S(2)}) copy-start(s32[128]{0:T(128)} %param.6) | copy-start | bytes 1540
  55.2 22.3 %collective-permute-start = (bf16[32,2,1280]{2,0,1:T(8,128)(2,1)}, bf16[32,2,1280]{2,0,1:T(8,128)(2,1)}, u32[]{:S(2)}, u32[]{:S(2)}) collective-permute-start(bf16[32,2,1280]{2,0,1:T(8,128)(2,1)} %get-tuple-element.65), channel_id=1, source_target_pairs={{0,1},{1,0},{2,3},{3,2},{4,5},{5,4},{6,7},{7,6},{8,9},{9,8},{10,11... | collective-permute-start | bytes 491528 | tf_op jit(solution)/shard_map/ppermute | solution.py:93
  55.2 24.6 %collective-permute-start.1 = (bf16[32,2,1280]{2,0,1:T(8,128)(2,1)}, bf16[32,2,1280]{2,0,1:T(8,128)(2,1)}, u32[]{:S(2)}, u32[]{:S(2)}) collective-permute-start(bf16[32,2,1280]{2,0,1:T(8,128)(2,1)} %get-tuple-element.64), channel_id=1, source_target_pairs={{0,2},{1,3},{2,0},{3,1},{4,6},{5,7},{6,4},{7,5},{8,10},{9,11},{10,... | collective-permute-start | bytes 491528 | tf_op jit(solution)/shard_map/ppermute | solution.py:93
  56.7 25.4 %collective-permute-start.2 = (bf16[32,2,1280]{2,0,1:T(8,128)(2,1)S(1)}, bf16[32,2,1280]{2,0,1:T(8,128)(2,1)}, u32[]{:S(2)}, u32[]{:S(2)}) collective-permute-start(bf16[32,2,1280]{2,0,1:T(8,128)(2,1)S(1)} %get-tuple-element.63), channel_id=1, source_target_pairs={{0,3},{1,2},{2,1},{3,0},{4,7},{5,6},{6,5},{7,4},{8,11},{9,10},{10,... | collective-permute-start | bytes 491528 | tf_op jit(solution)/shard_map/ppermute | solution.py:93
  84.5 1.5 %copy-start = (bf16[32,8,1280]{0,1,2:T(8,128)(2,1)}, bf16[32,8,1280]{0,1,2:T(8,128)(2,1)S(1)}, u32[]{:S(2)}) copy-start(bf16[32,8,1280]{0,1,2:T(8,128)(2,1)S(1)} %get-tuple-element.119) | copy-start | bytes 1966084 | tf_op jit(solution)/shard_map/while
  103.8 3.1 %copy-start.2 = (f32[8,32,640]{2,1,0:T(8,128)S(1)}, f32[8,32,640]{2,1,0:T(8,128)}, u32[]{:S(2)}) copy-start(f32[8,32,640]{2,1,0:T(8,128)} %copy.67) | copy-start | bytes 1966084 | tf_op jit(solution)/shard_map/while
  106.9 5.8 %copy-start.1 = (bf16[32,8,1280]{0,1,2:T(8,128)(2,1)S(1)}, bf16[32,8,1280]{0,1,2:T(8,128)(2,1)}, u32[]{:S(2)}) copy-start(bf16[32,8,1280]{0,1,2:T(8,128)(2,1)} %copy-done) | copy-start | bytes 1966084 | tf_op jit(solution)/shard_map/while
  112.7 1.5 %copy-start = (bf16[32,8,1280]{0,1,2:T(8,128)(2,1)}, bf16[32,8,1280]{0,1,2:T(8,128)(2,1)S(1)}, u32[]{:S(2)}) copy-start(bf16[32,8,1280]{0,1,2:T(8,128)(2,1)S(1)} %get-tuple-element.119) | copy-start | bytes 1966084 | tf_op jit(solution)/shard_map/while
  131.9 3.1 %copy-start.2 = (f32[8,32,640]{2,1,0:T(8,128)S(1)}, f32[8,32,640]{2,1,0:T(8,128)}, u32[]{:S(2)}) copy-start(f32[8,32,640]{2,1,0:T(8,128)} %copy.67) | copy-start | bytes 1966084 | tf_op jit(solution)/shard_map/while
  135.1 5.8 %copy-start.1 = (bf16[32,8,1280]{0,1,2:T(8,128)(2,1)S(1)}, bf16[32,8,1280]{0,1,2:T(8,128)(2,1)}, u32[]{:S(2)}) copy-start(bf16[32,8,1280]{0,1,2:T(8,128)(2,1)} %copy-done) | copy-start | bytes 1966084 | tf_op jit(solution)/shard_map/while
